TPU v7x, 32 devices: a whole 2x2x4 slice. The times are simulated.
32 devices in a mesh: dp: 8 (over z, x), tensor: 4 (over y, core).
Axes of the slice: x: 2, y: 2, z: 4, core: 2. Of those that a mesh axis runs over, the one named last changes fastest.
Arguments:
- layer_input: bfloat16 [4096, 768], P('dp', 'tensor'), may hold values from -6 to 6
- segment_ids: int32 [8, 512], P('dp'), may hold values from 0 to 15, never falling along the last dimension, each value on 1 to 256 neighbouring positions
- triple_weight: bfloat16 [768, 3, 768], P(None, None, 'tensor'), may hold values from -0.21875 to 0.21875
- query_value_bias: float32 [2, 768], P(None, 'tensor'), may hold values from -3 to 3
- output_weight: bfloat16 [768, 768], P('tensor'), may hold values from -0.875 to 0.875
- output_bias: float32 [768], P('tensor'), may hold values from -3 to 3
- norm_gain: float32 [768], P('tensor'), may hold values from 0.5 to 1.5
- norm_shift: float32 [768], P('tensor'), may hold values from -3 to 3
- expand_weight: bfloat16 [768, 3072], P(None, 'tensor'), may hold values from -0.21875 to 0.21875
- expand_bias: float32 [3072], P('tensor'), may hold values from -3 to 3
- reduce_weight: bfloat16 [3072, 768], P('tensor'), may hold values from -0.109375 to 0.109375
- reduce_bias: float32 [768], P('tensor'), may hold values from -3 to 3
- final_gain: float32 [768], P('tensor'), may hold values from 0.5 to 1.5
- final_shift: float32 [768], P('tensor'), may hold values from -3 to 3
- cotangent: bfloat16 [4096, 768], P('dp', 'tensor'), may hold values from -6 to 6
Outputs:
- layer_output: bfloat16 [4096, 768], P('dp', 'tensor')
- input_grad: float32 [4096, 768], P('dp', 'tensor')
- triple_grad: float32 [768, 3, 768], P(None, None, 'tensor')
- query_value_grad: float32 [2, 768], P(None, 'tensor')
- output_weight_grad: float32 [768, 768], P('tensor')
- output_bias_grad: float32 [768], P('tensor')
- norm_gain_grad: float32 [768], P('tensor')
- norm_shift_grad: float32 [768], P('tensor')
- expand_weight_grad: float32 [768, 3072], P(None, 'tensor')
- expand_bias_grad: float32 [3072], P('tensor')
- reduce_weight_grad: float32 [3072, 768], P('tensor')
- reduce_bias_grad: float32 [768], P('tensor')
- final_gain_grad: float32 [768], P('tensor')
- final_shift_grad: float32 [768], P('tensor')
Inputs may be any that keep to these rules, and one draw needn't show every extreme that they name: `segment_ids`: segment numbers never fall along a sequence; each document holds 1 to 256 tokens.
All inputs are finite; a program needn't handle non-finite values.
Results may differ from a plain program's by a relative error of at most 0.012.
The roundings to bfloat16 on the way count: a program that leaves them out, or rounds other values in their place, can miss the bound.
Values may be sent and summed in bfloat16 or wider, within the bound.
A program may use at most 64 MiB of HBM per device.

v0:
```python
import jax
import jax.numpy as jnp
from jax import lax
from jax.sharding import PartitionSpec as P

D = 768
HD = 64
EPS = 1e-06


def gelu_value(pre_act):
    return 0.5 * pre_act * (1.0 + lax.erf(pre_act * 0.7071067811865476))


def gelu_slope(pre_act):
    return (
        0.5 * (1.0 + lax.erf(pre_act * 0.7071067811865476))
        + pre_act * jnp.exp(-0.5 * pre_act * pre_act) * 0.3989422804014327
    )


def norm_forward(hidden, gain, shift):
    row_mean = jnp.mean(hidden, axis=-1, keepdims=True)
    centred = hidden - row_mean
    inverse = lax.rsqrt(jnp.mean(centred * centred, axis=-1, keepdims=True) + EPS)
    normed = centred * inverse
    return (normed * gain + shift, normed, inverse)


def norm_backward(upstream, normed, inverse, gain):
    scaled = upstream * gain
    first_mean = jnp.mean(scaled, axis=-1, keepdims=True)
    second_mean = jnp.mean(scaled * normed, axis=-1, keepdims=True)
    return inverse * (scaled - first_mean - normed * second_mean)


def sum_rows(partial):
    return lax.psum_scatter(
        partial.astype(jnp.bfloat16), "tensor", scatter_dimension=0, tiled=True
    ).astype(jnp.float32)


def all_rows(piece):
    return lax.all_gather(piece, "tensor", axis=0, tiled=True)


def column_sum(rows):
    return jnp.sum(rows, axis=0)


def tall_dot(left, right):
    return lax.dot_general(
        left, right, (((0,), (0,)), ((), ())), preferred_element_type=jnp.float32
    )


def wide_dot(left, right):
    return lax.dot_general(
        left, right, (((1,), (1,)), ((), ())), preferred_element_type=jnp.float32
    )


def masked_scores(query_part, key_part, segment_row, head_scale):
    scores = (
        jnp.einsum("qhd,khd->hqk", query_part, key_part, preferred_element_type=jnp.float32)
        * head_scale
    )
    allowed = segment_row[:, None] == segment_row[None, :]
    return jnp.where(allowed[None], scores, -jnp.inf)


def per_device(
    layer_input,
    segment_ids,
    triple_weight,
    query_value_bias,
    output_weight,
    output_bias,
    norm_gain,
    norm_shift,
    expand_weight,
    expand_bias,
    reduce_weight,
    reduce_bias,
    final_gain,
    final_shift,
    cotangent,
):
    seq_len = segment_ids.shape[1]
    tok_count = segment_ids.shape[0] * seq_len
    local_width = triple_weight.shape[2]
    local_heads = local_width // HD
    head_scale = HD ** (-0.5)
    groups = lax.axis_size("tensor")
    rank = lax.axis_index("tensor")
    block = tok_count // groups
    both = lax.all_gather(
        jnp.concatenate([layer_input, cotangent], axis=0), "tensor", axis=1, tiled=True
    )
    gathered = both[:tok_count]
    own_input = lax.dynamic_slice_in_dim(both, rank * block, block, 0).astype(jnp.float32)
    upstream = lax.dynamic_slice_in_dim(both, tok_count + rank * block, block, 0).astype(
        jnp.float32
    )
    vectors = lax.all_gather(
        jnp.stack([output_bias, norm_gain, norm_shift, reduce_bias, final_gain, final_shift]),
        "tensor",
        axis=1,
        tiled=True,
    )
    output_bias, norm_gain, norm_shift, reduce_bias, final_gain, final_shift = [
        vectors[i] for i in range(6)
    ]
    projected = jnp.einsum(
        "td,dcf->tcf", gathered, triple_weight, preferred_element_type=jnp.float32
    )
    query_half = (
        (projected[:, 0] + query_value_bias[0])
        .astype(jnp.bfloat16)
        .reshape(seq_len, local_heads, HD)
    )
    key_half = projected[:, 1].astype(jnp.bfloat16).reshape(seq_len, local_heads, HD)
    value_half = (
        (projected[:, 2] + query_value_bias[1])
        .astype(jnp.bfloat16)
        .reshape(seq_len, local_heads, HD)
    )
    scores = masked_scores(query_half, key_half, segment_ids[0], head_scale)
    top = jnp.max(scores, axis=-1, keepdims=True)
    log_total = top + jnp.log(jnp.sum(jnp.exp(scores - top), axis=-1, keepdims=True))
    probs_half = jnp.exp(scores - log_total).astype(jnp.bfloat16)
    context = jnp.einsum(
        "hqk,khd->qhd", probs_half, value_half, preferred_element_type=jnp.float32
    ).astype(jnp.bfloat16)
    context_flat = context.reshape(tok_count, local_width)
    first_sum = (
        own_input
        + sum_rows(jnp.dot(context_flat, output_weight, preferred_element_type=jnp.float32))
        + output_bias
    )
    attended, normed_one, inv_one = norm_forward(first_sum, norm_gain, norm_shift)
    attended_half = all_rows(attended.astype(jnp.bfloat16))
    pre_act = (
        jnp.dot(attended_half, expand_weight, preferred_element_type=jnp.float32) + expand_bias
    )
    activated = gelu_value(pre_act).astype(jnp.bfloat16)
    second_sum = (
        attended
        + sum_rows(jnp.dot(activated, reduce_weight, preferred_element_type=jnp.float32))
        + reduce_bias
    )
    out_f, normed_two, inv_two = norm_forward(second_sum, final_gain, final_shift)
    layer_output = lax.all_to_all(
        out_f.astype(jnp.bfloat16), "tensor", split_axis=1, concat_axis=0, tiled=True
    )
    final_gain_grad = column_sum(upstream * normed_two)
    final_shift_grad = column_sum(upstream)
    second_grad = norm_backward(upstream, normed_two, inv_two, final_gain)
    second_half = all_rows(second_grad.astype(jnp.bfloat16))
    reduce_weight_grad = tall_dot(activated, second_half)
    reduce_bias_grad = column_sum(second_grad)
    act_grad = wide_dot(second_half, reduce_weight) * gelu_slope(pre_act)
    act_half = act_grad.astype(jnp.bfloat16)
    expand_weight_grad = tall_dot(attended_half, act_half)
    expand_bias_grad = column_sum(act_grad)
    feed_sum = lax.psum(
        jnp.concatenate([reduce_weight_grad, expand_weight_grad], axis=0).astype(jnp.bfloat16), "dp"
    )
    split = reduce_weight_grad.shape[0]
    attended_grad = second_grad + sum_rows(wide_dot(act_half, expand_weight))
    norm_gain_grad = column_sum(attended_grad * normed_one)
    norm_shift_grad = column_sum(attended_grad)
    first_grad = norm_backward(attended_grad, normed_one, inv_one, norm_gain)
    first_half = all_rows(first_grad.astype(jnp.bfloat16))
    output_weight_grad = tall_dot(context_flat, first_half)
    output_bias_grad = column_sum(first_grad)
    grad_part = (
        wide_dot(first_half, output_weight).astype(jnp.bfloat16).reshape(seq_len, local_heads, HD)
    )
    scores = masked_scores(query_half, key_half, segment_ids[0], head_scale)
    probs = jnp.exp(scores - log_total)
    probs_half = probs.astype(jnp.bfloat16)
    value_grad = jnp.einsum(
        "hqk,qhd->khd", probs_half, grad_part, preferred_element_type=jnp.float32
    ).reshape(tok_count, local_width)
    prob_grad = jnp.einsum(
        "qhd,khd->hqk", grad_part, value_half, preferred_element_type=jnp.float32
    )
    delta = jnp.einsum("qhd,qhd->hq", grad_part.astype(jnp.float32), context.astype(jnp.float32))
    score_grad = (probs * (prob_grad - delta[:, :, None]) * head_scale).astype(jnp.bfloat16)
    query_grad = jnp.einsum(
        "hqk,khd->qhd", score_grad, key_half, preferred_element_type=jnp.float32
    ).reshape(tok_count, local_width)
    key_grad = jnp.einsum(
        "hqk,qhd->khd", score_grad, query_half, preferred_element_type=jnp.float32
    ).reshape(tok_count, local_width)
    triple_half = jnp.stack([query_grad, key_grad, value_grad], axis=1).astype(jnp.bfloat16)
    triple_grad = jnp.einsum(
        "td,tcf->dcf", gathered, triple_half, preferred_element_type=jnp.float32
    )
    input_terms = jnp.einsum(
        "tcf,dcf->td", triple_half, triple_weight, preferred_element_type=jnp.float32
    )
    smalls = jnp.stack(
        [
            output_bias_grad,
            norm_gain_grad,
            norm_shift_grad,
            reduce_bias_grad,
            final_gain_grad,
            final_shift_grad,
        ]
    )
    own_rows = lax.dynamic_slice_in_dim(input_terms, rank * block, block, 0) + first_grad
    input_terms = lax.dynamic_update_slice_in_dim(input_terms, own_rows, rank * block, 0)
    shares = lax.psum_scatter(
        jnp.concatenate([input_terms, smalls, jnp.zeros((10, D), jnp.float32)], axis=0).astype(
            jnp.bfloat16
        ),
        "tensor",
        scatter_dimension=1,
        tiled=True,
    ).astype(jnp.float32)
    input_grad = shares[:tok_count]
    pieces = [
        triple_grad,
        output_weight_grad,
        expand_bias_grad,
        jnp.sum(query_grad, axis=0),
        jnp.sum(value_grad, axis=0),
        shares[tok_count : tok_count + 6],
    ]
    packed = jnp.concatenate([p.reshape(-1, local_width) for p in pieces], axis=0)
    packed, feed_sum = lax.optimization_barrier((packed.astype(jnp.bfloat16), feed_sum))
    packed = lax.psum(packed, "dp").astype(jnp.float32)
    reduce_weight_grad = feed_sum[:split].astype(jnp.float32)
    expand_weight_grad = feed_sum[split:].astype(jnp.float32)
    outs, at = ([], 0)
    for p in pieces:
        count = p.size // local_width
        outs.append(packed[at : at + count].reshape(p.shape))
        at += count
    triple_grad, output_weight_grad, expand_bias_grad, query_sum, value_sum, small_sums = outs
    return (
        layer_output,
        input_grad,
        triple_grad,
        jnp.stack([query_sum, value_sum]),
        output_weight_grad,
        small_sums[0],
        small_sums[1],
        small_sums[2],
        expand_weight_grad,
        expand_bias_grad,
        reduce_weight_grad,
        small_sums[3],
        small_sums[4],
        small_sums[5],
    )


def solution(mesh):
    in_specs = (
        P("dp", "tensor"),
        P("dp", None),
        P(None, None, "tensor"),
        P(None, "tensor"),
        P("tensor", None),
        P("tensor"),
        P("tensor"),
        P("tensor"),
        P(None, "tensor"),
        P("tensor"),
        P("tensor", None),
        P("tensor"),
        P("tensor"),
        P("tensor"),
        P("dp", "tensor"),
    )
    out_specs = (
        P("dp", "tensor"),
        P("dp", "tensor"),
        P(None, None, "tensor"),
        P(None, "tensor"),
        P("tensor", None),
        P("tensor"),
        P("tensor"),
        P("tensor"),
        P(None, "tensor"),
        P("tensor"),
        P("tensor", None),
        P("tensor"),
        P("tensor"),
        P("tensor"),
    )
    return jax.shard_map(
        per_device, mesh=mesh, in_specs=in_specs, out_specs=out_specs, check_vma=False
    )
```

profile of v0, /device:TPU:0, one launch (start us, length us, event | category | flops | bytes accessed | tf_op | source)
XLA Modules:
  0.0 413.7 jit_solution(5651966376495020116)
XLA Ops:
  7.2 1.9 pad_maximum_fusion.2
  9.2 0.8 slice_reduce_fusion.6
  10.2 1.0 broadcast_compare_fusion
  11.1 21.4 %all-gather.3.cloned.1.call-done = bf16[1024,768]{0,1:T(8,128)(2,1)} async-done(((bf16[1024,192]{0,1:T(8,128)(2,1)}), bf16[1024,768]{0,1:T(8,128)(2,1)}) %all-gather.3.cloned.1.call-update) | async-done | bytes 1572880 | tf_op jit(solution)/shard_map/all_gather | solution.py:97
  32.6 2.0 fusion.7
  34.7 0.8 fusion.1
  35.5 0.7 exponential_reduce_fusion
  36.2 0.9 copy-done.1
  37.1 1.0 convolution_convert_fusion.7
  38.2 1.3 convolution_convert_fusion.4
  39.7 5.2 %all-gather = f32[4,192,6]{1,2,0:T(8,128)S(1)} all-gather(f32[1,192,6]{1,2,0:T(8,128)S(1)} %bitcast.109), channel_id=1, replica_groups=mesh['dp'=8,'tensor'=4] {'tensor'}, dimensions={0}, use_global_device_ids=true | all-gather | bytes 23040 | tf_op jit(solution)/shard_map/all_gather | solution.py:105
  45.0 1.2 fusion.27
  46.4 16.6 %reduce-scatter.7.cloned.1.call-done = bf16[128,768]{1,0:T(8,128)(2,1)} async-done(((bf16[512,768]{1,0:T(8,128)(2,1)}), bf16[128,768]{1,0:T(8,128)(2,1)}) %reduce-scatter.7.cloned.1.call-update) | async-done | bytes 196624 | tf_op jit(solution)/shard_map/reduce_scatter | solution.py:38
  63.0 1.1 fusion.22
  64.0 1.1 multiply_reduce_fusion.3
  65.2 1.1 fusion.21
  66.2 8.2 %all_gather.17 = bf16[512,768]{1,0:T(8,128)(2,1)S(1)} all-gather(bf16[128,768]{1,0:T(8,128)(2,1)S(1)} %fusion.21), channel_id=1, replica_groups=mesh['dp'=8,'tensor'=4] {'tensor'}, dimensions={0}, use_global_device_ids=true | all-gather | bytes 983040 | tf_op jit(solution)/shard_map/all_gather | solution.py:44
  74.5 2.0 multiply_convert_fusion.1
  76.5 0.9 copy-done.30
  77.4 1.7 convolution_convert_fusion.3
  79.3 23.6 %reduce-scatter.9.cloned.1.call-done = bf16[128,768]{1,0:T(8,128)(2,1)} async-done(((bf16[512,768]{1,0:T(8,128)(2,1)}), bf16[128,768]{1,0:T(8,128)(2,1)}) %reduce-scatter.9.cloned.1.call-update) | async-done | bytes 196624 | tf_op jit(solution)/shard_map/reduce_scatter | solution.py:38
  102.9 1.2 fusion.31
  104.6 0.9 fusion.29
  105.5 8.2 %all_gather.18 = bf16[512,768]{1,0:T(8,128)(2,1)S(1)} all-gather(bf16[128,768]{1,0:T(8,128)(2,1)S(1)} %get-tuple-element.94), channel_id=1, replica_groups=mesh['dp'=8,'tensor'=4] {'tensor'}, dimensions={0}, use_global_device_ids=true | all-gather | bytes 983040 | tf_op jit(solution)/shard_map/all_gather | solution.py:44
  113.7 1.7 fusion.36
  115.4 0.9 copy-done.31
  116.2 1.7 convolution_convert_fusion.2
  118.0 23.7 %reduce-scatter.11.cloned.1.call-done = bf16[128,768]{1,0:T(8,128)(2,1)} async-done(((bf16[512,768]{1,0:T(8,128)(2,1)}), bf16[128,768]{1,0:T(8,128)(2,1)}) %reduce-scatter.11.cloned.1.call-update) | async-done | bytes 196624 | tf_op jit(solution)/shard_map/reduce_scatter | solution.py:38
  141.8 1.3 multiply_reduce_fusion
  143.1 1.2 fusion.28
  144.3 8.5 %all_gather.19 = bf16[512,768]{1,0:T(8,128)(2,1)S(1)} all-gather(bf16[128,768]{1,0:T(8,128)(2,1)S(1)} %convert_element_type.106), channel_id=1, replica_groups=mesh['dp'=8,'tensor'=4] {'tensor'}, dimensions={0}, use_global_device_ids=true | all-gather | bytes 983040 | tf_op jit(solution)/shard_map/all_gather | solution.py:44
  153.4 1.4 multiply_convert_fusion
  155.8 1.7 fusion.34
  157.5 0.8 convolution_bitcast_fusion
  158.4 1.0 convert.78
  159.4 3.1 concatenate.16
  162.5 1.3 copy.87
  163.9 2.3 convolution_convert_fusion.1
  166.2 0.8 convolution_convert_fusion
  167.0 1.6 pad_maximum_fusion
  168.7 0.6 copy-done.19
  169.4 1.2 pad_maximum_fusion.1
  170.6 0.7 fusion.9
  171.2 1.0 convert.85
  172.2 2.5 copy.72
  174.8 2.2 reshape.172
  177.0 1.3 convolution_convert_fusion.5
  178.9 10.0 %reduce-scatter.13.cloned.1.call-done = bf16[192,528]{1,0:T(8,128)(2,1)} async-done(((bf16[768,528]{1,0:T(8,128)(2,1)}), bf16[192,528]{1,0:T(8,128)(2,1)}) %reduce-scatter.13.cloned.1.call-update) | async-done | bytes 202768
  188.9 0.8 slice.127
  189.8 6.7 %concatenate.17 = bf16[3084,192]{1,0:T(8,128)(2,1)} concatenate(bf16[2304,192]{1,0:T(8,128)(2,1)S(1)} %copy-done.5, bf16[768,192]{1,0:T(8,128)(2,1)S(1)} %reshape.173, bf16[4,192]{1,0:T(4,128)(2,1)S(1)} %reshape.174, bf16[1,192]{1,0:T(2,128)(2,1)S(1)} %reshape.175, bf16[1,192]{1,0:T(2,128)(2,1)S(1)} %reshape.176, bf16[6,192]{1,0:T(8,128)(2,1)S(1)} %copy.93), dimensions={0} | concatenate | bytes 2368512 | tf_op jit(solution)/shard_map/concatenate | solution.py:233
  196.5 105.1 %all-reduce.3.cloned.1.call-done = bf16[1536,768]{1,0:T(8,128)(2,1)} async-done(((bf16[1536,768]{1,0:T(8,128)(2,1)}), bf16[1536,768]{1,0:T(8,128)(2,1)}) %all-reduce.3.cloned.1.call-update) | async-done | bytes 2359312 | tf_op jit(solution)/shard_map/psum | solution.py:166
  301.7 1.9 copy.65
  303.6 8.7 %all_to_all.19 = bf16[128,4,192]{0,2,1:T(8,128)(2,1)S(1)} all-to-all(bf16[128,4,192]{0,2,1:T(8,128)(2,1)} %bitcast.101), channel_id=1, replica_groups=mesh['dp'=8,'tensor'=4] {'tensor'}, dimensions={1} | all-to-all | bytes 393216 | tf_op jit(solution)/shard_map/all_to_all | solution.py:153
  312.2 0.7 copy_bitcast_fusion
  312.9 1.6 slice.126
  314.5 1.8 copy.92
  316.3 1.8 copy.73
  318.1 2.5 slice_convert_fusion
  320.7 74.8 %all-reduce.5.cloned.1.call-done = bf16[3084,192]{1,0:T(8,128)(2,1)} async-done(((bf16[3084,192]{1,0:T(8,128)(2,1)}), bf16[3084,192]{1,0:T(8,128)(2,1)}) %all-reduce.5.cloned.1.call-update) | async-done | bytes 1184272 | tf_op jit(solution)/shard_map/psum | solution.py:235
  395.5 1.4 slice.128
  396.9 2.6 reshape.177
  399.5 4.3 %copy.74 = f32[768,3,192]{0,2,1:T(8,128)} copy(f32[768,3,192]{2,1,0:T(4,128)} %reshape.177) | data formatting | bytes 3538944
  403.9 1.1 reshape.178
  405.1 0.7 reshape.179
  (120 shorter events, 5.4 us)
Async XLA Ops:
  7.2 67.3 %copy-start = (bf16[768,768]{1,0:T(8,128)(2,1)S(1)}, bf16[768,768]{1,0:T(8,128)(2,1)}, u32[]{:S(2)}) copy-start(bf16[768,768]{1,0:T(8,128)(2,1)} %param.23) | copy-start | bytes 3538948
  7.2 25.4 %all-gather.3.cloned.1.call-start = ((), (), s32[]{:S(2)}) async-start(), calls=%async_computation.5 | async-start | bytes 1966080 | tf_op jit(solution)/shard_map/all_gather | solution.py:97
  9.2 53.8 %reduce-scatter.7.cloned.1.call-start = ((), (), s32[]{:S(2)}) async-start(), calls=%async_computation.6 | async-start | bytes 983040 | tf_op jit(solution)/shard_map/reduce_scatter | solution.py:38
  34.6 1.6 copy-start.16
  35.5 1.7 copy-start.1
  37.1 1.1 copy-start.9
  38.1 115.1 %copy-start.8 = (bf16[3,64,512]{2,1,0:T(8,128)(2,1)}, bf16[3,64,512]{2,1,0:T(8,128)(2,1)S(1)}, u32[]{:S(2)}) copy-start(bf16[3,64,512]{2,1,0:T(8,128)(2,1)S(1)} %convolution_convert_fusion.7) | copy-start | bytes 589828
  38.1 1.5 copy-start.20
  38.2 1.5 copy-start.21
  38.2 1.5 copy-start.22
  38.2 1.4 copy-start.23
  38.2 1.4 copy-start.24
  38.2 1.4 copy-start.25
  39.5 63.4 %reduce-scatter.9.cloned.1.call-start = ((), (), s32[]{:S(2)}) async-start(), calls=%async_computation.7 | async-start | bytes 983040 | tf_op jit(solution)/shard_map/reduce_scatter | solution.py:38
  46.2 28.2 %copy-start.29 = (f32[768]{0:T(1024)S(1)}, f32[768]{0:T(1024)}, u32[]{:S(2)}) copy-start(f32[768]{0:T(1024)} %param.24) | copy-start | bytes 9220
  74.5 2.0 copy-start.13
  74.5 3.0 copy-start.27
  76.5 0.9 copy-start.30
  77.4 25.5 %copy-start.3 = (bf16[128,768]{1,0:T(8,128)(2,1)S(1)}, bf16[128,768]{1,0:T(8,128)(2,1)}, u32[]{:S(2)}) copy-start(bf16[128,768]{1,0:T(8,128)(2,1)} %reduce-scatter.7.cloned.1.call-done) | copy-start | bytes 589828
  79.1 62.7 %reduce-scatter.11.cloned.1.call-start = ((), (), s32[]{:S(2)}) async-start(), calls=%async_computation.8 | async-start | bytes 983040 | tf_op jit(solution)/shard_map/reduce_scatter | solution.py:38
  104.3 9.4 %copy-start.28 = (bf16[768,768]{1,0:T(8,128)(2,1)S(1)}, bf16[768,768]{1,0:T(8,128)(2,1)}, u32[]{:S(2)}) copy-start(bf16[768,768]{1,0:T(8,128)(2,1)} %param.25) | copy-start | bytes 3538948
  104.3 9.4 %copy-start.33 = (f32[512,768]{1,0:T(8,128)S(1)}, f32[512,768]{1,0:T(8,128)}, u32[]{:S(2)}) copy-start(f32[512,768]{1,0:T(8,128)} %get-tuple-element.117) | copy-start | bytes 4718596
  113.7 1.7 copy-start.15
  115.4 0.9 copy-start.31
  118.0 70.9 %reduce-scatter.13.cloned.1.call-start = ((), (), s32[]{:S(2)}) async-start(), calls=%async_computation.11 | async-start | bytes 1228800
  143.1 10.3 %copy-start.17 = (f32[512,1,192]{0,2,1:T(8,128)S(1)}, f32[512,1,192]{0,2,1:T(8,128)}, u32[]{:S(2)}) copy-start(f32[512,1,192]{0,2,1:T(8,128)} %copy-done.16) | copy-start | bytes 1179652
  144.3 9.1 %copy-start.2 = (f32[3,512,512]{1,2,0:T(8,128)S(1)}, f32[3,512,512]{1,2,0:T(8,128)}, u32[]{:S(2)}) copy-start(f32[3,512,512]{1,2,0:T(8,128)} %copy-done.1) | copy-start | bytes 9437188
  155.2 2.3 copy-start.11
  155.8 1.7 copy-start.12
  155.8 1.7 copy-start.10
  157.5 0.8 copy-start.18
  163.8 2.4 copy-start.14
  163.9 2.4 copy-start.32
  163.9 137.8 %all-reduce.3.cloned.1.call-start = ((), (), s32[]{:S(2)}) async-start(), calls=%async_computation.9 | async-start | bytes 4718592 | tf_op jit(solution)/shard_map/psum | solution.py:166
  168.6 0.7 copy-start.19
  168.6 2.0 copy-start.6
  168.6 226.9 %all-reduce.5.cloned.1.call-start = ((), (), s32[]{:S(2)}) async-start(), calls=%async_computation.10 | async-start | bytes 3162112 | tf_op jit(solution)/shard_map/psum | solution.py:235
  177.0 1.8 copy-start.26
  177.0 12.8 %copy-start.5 = (bf16[2304,192]{1,0:T(8,128)(2,1)S(1)}, bf16[2304,192]{1,0:T(8,128)(2,1)}, u32[]{:S(2)}) copy-start(bf16[2304,192]{1,0:T(8,128)(2,1)} %reshape.172) | copy-start | bytes 2654212
  301.7 16.5 %copy-start.7 = (bf16[1536,768]{1,0:T(8,128)(2,1)S(1)}, bf16[1536,768]{1,0:T(8,128)(2,1)}, u32[]{:S(2)}) copy-start(bf16[1536,768]{1,0:T(8,128)(2,1)} %all-reduce.3.cloned.1.call-done) | copy-start | bytes 7077892
  399.5 4.3 %copy-start.4 = (bf16[3084,192]{1,0:T(8,128)(2,1)S(1)}, bf16[3084,192]{1,0:T(8,128)(2,1)}, u32[]{:S(2)}) copy-start(bf16[3084,192]{1,0:T(8,128)(2,1)} %all-reduce.5.cloned.1.call-done) | copy-start | bytes 3552772
Sparse Core Ops, SparseCore 0:
  10.2 22.3 all-gather.2
  39.7 23.2 reduce-scatter.6
  79.2 23.6 reduce-scatter.8
  118.1 23.6 reduce-scatter.10
  164.0 24.8 reduce-scatter.12
  192.9 108.7 all-reduce.2
  306.2 89.2 all-reduce.4
where the time goes:
time: 415 us; the launch traced here: 414 us
  waiting for transfers between devices  275 us (66%)
  local copies, waits for them, and re-layouts  41.6 us (10%)
  blocking collectives  38.8 us (9%)
  matrix products  22.5 us (5%)
  other arithmetic  20.5 us (5%)
  between operations  14.7 us (4%)
    psum x1, waiting for transfers between devices, per_device(): lax.psum(jnp.concatenate([reduce_weight_grad, expand_weight_grad], axis=0...  105 us
    psum x1, waiting for transfers between devices, per_device(): packed = lax.psum(packed, 'dp').astype(jnp.float32)  74.8 us
    reduce_scatter x3, waiting for transfers between devices, sum_rows(): lax.psum_scatter(partial.astype(jnp.bfloat16), 'tensor', scatter_dimensio...  63.9 us
    all_gather x3, blocking collectives, all_rows(): return lax.all_gather(piece, 'tensor', axis=0, tiled=True)  24.9 us
    all_gather x1, waiting for transfers between devices, per_device(): lax.all_gather(jnp.concatenate([layer_input, cotangent], axis=0), 'tensor...  21.4 us
    unnamed x76, local copies, waits for them, and re-layouts  13.2 us
    unnamed x8, waiting for transfers between devices  10.1 us
    all_to_all x1, blocking collectives, per_device(): lax.all_to_all(out_f.astype(jnp.bfloat16), 'tensor', split_axis=1, concat...  8.67 us
  transfers between devices with their start and end apart: 7, of which 7 were waited for; matrix products, arithmetic and copies ran while one was open for 9% of the time, Pallas kernels for 0%

commit v1 on v0

--- a/solution.py
+++ b/solution.py
@@ -232,7 +232,7 @@
     ]
     packed = jnp.concatenate([p.reshape(-1, local_width) for p in pieces], axis=0)
     packed, feed_sum = lax.optimization_barrier((packed.astype(jnp.bfloat16), feed_sum))
-    packed = lax.psum(packed, "dp").astype(jnp.float32)
+    packed = jnp.sum(lax.all_gather(packed, "dp"), axis=0).astype(jnp.float32)
     reduce_weight_grad = feed_sum[:split].astype(jnp.float32)
     expand_weight_grad = feed_sum[split:].astype(jnp.float32)
     outs, at = ([], 0)

time: 415 us -> 474 us (1.14)
  waiting for transfers between devices: 275 us -> 342 us
  local copies, waits for them, and re-layouts: 41.6 us -> 30.5 us
  other arithmetic: 20.5 us -> 25.9 us
    all_gather x0 -> x1, waiting for transfers between devices: none -> 131 us  [per_device(): packed = jnp.sum(lax.all_gather(packed, 'dp'), axis=0).astype(jnp.float32)]
    psum x1 -> x0, waiting for transfers between devices: 74.8 us -> none  [per_device(): packed = lax.psum(packed, 'dp').astype(jnp.float32)]
    psum x1, waiting for transfers between devices: 105 us -> 111 us  [per_device(): lax.psum(jnp.concatenate([reduce_weight_grad, expand_weight_grad], axis=0...]
    concatenate x1, local copies, waits for them, and re-layouts: 6.74 us -> 0.55 us  [per_device(): jnp.concatenate([p.reshape(-1, local_width) for p in pieces], axis=0)]
    reduce_sum x0 -> x1, other arithmetic: none -> 5.83 us  [per_device(): packed = jnp.sum(lax.all_gather(packed, 'dp'), axis=0).astype(jnp.float32)]
    unnamed x76 -> x84, local copies, waits for them, and re-layouts: 13.2 us -> 13 us
  transfers between devices with their start and end apart: 7 -> 7, of which waited for: 7 -> 7; matrix products, arithmetic and copies ran while one was open for 9% -> 4% of each run, Pallas kernels for 0% -> 0%
where the time goes in v1:
time: 474 us; the launch traced here: 473 us
  waiting for transfers between devices  342 us (72%)
  blocking collectives  38.1 us (8%)
  local copies, waits for them, and re-layouts  30.5 us (6%)
  other arithmetic  25.9 us (5%)
  matrix products  21.9 us (5%)
  between operations  14.8 us (3%)
    all_gather x1, waiting for transfers between devices, per_device(): packed = jnp.sum(lax.all_gather(packed, 'dp'), axis=0).astype(jnp.float32)  131 us
    psum x1, waiting for transfers between devices, per_device(): lax.psum(jnp.concatenate([reduce_weight_grad, expand_weight_grad], axis=0...  111 us
    reduce_scatter x3, waiting for transfers between devices, sum_rows(): lax.psum_scatter(partial.astype(jnp.bfloat16), 'tensor', scatter_dimensio...  63.9 us
    all_gather x3, blocking collectives, all_rows(): return lax.all_gather(piece, 'tensor', axis=0, tiled=True)  24.9 us
    all_gather x1, waiting for transfers between devices, per_device(): lax.all_gather(jnp.concatenate([layer_input, cotangent], axis=0), 'tensor...  21.4 us
    unnamed x8, waiting for transfers between devices  14.4 us
    unnamed x84, local copies, waits for them, and re-layouts  13 us
  transfers between devices with their start and end apart: 7, of which 7 were waited for; matrix products, arithmetic and copies ran while one was open for 4% of the time, Pallas kernels for 0%

profile of v1, /device:TPU:0, one launch (start us, length us, event | category | flops | bytes accessed | tf_op | source)
XLA Modules:
  0.0 473.2 jit_solution(12467113648468604102)
XLA Ops:
  7.2 1.9 pad_maximum_fusion.2
  9.2 0.8 slice_reduce_fusion.12
  10.2 1.0 broadcast_compare_fusion
  11.1 21.4 %all-gather.6.cloned.1.call-done = bf16[1024,768]{0,1:T(8,128)(2,1)} async-done(((bf16[1024,192]{0,1:T(8,128)(2,1)}), bf16[1024,768]{0,1:T(8,128)(2,1)}) %all-gather.6.cloned.1.call-update) | async-done | bytes 1572880 | tf_op jit(solution)/shard_map/all_gather | solution.py:97
  32.6 2.0 fusion.7
  34.7 0.8 fusion.1
  35.5 0.7 exponential_reduce_fusion
  36.2 0.9 copy-done.2
  37.1 1.0 convolution_convert_fusion.7
  38.2 1.3 convolution_convert_fusion.4
  39.7 5.2 %all-gather.1 = f32[4,192,6]{1,2,0:T(8,128)S(1)} all-gather(f32[1,192,6]{1,2,0:T(8,128)S(1)} %bitcast.105), channel_id=1, replica_groups=mesh['dp'=8,'tensor'=4] {'tensor'}, dimensions={0}, use_global_device_ids=true | all-gather | bytes 23040 | tf_op jit(solution)/shard_map/all_gather | solution.py:105
  45.0 1.2 fusion.27
  46.4 16.6 %reduce-scatter.7.cloned.1.call-done = bf16[128,768]{1,0:T(8,128)(2,1)} async-done(((bf16[512,768]{1,0:T(8,128)(2,1)}), bf16[128,768]{1,0:T(8,128)(2,1)}) %reduce-scatter.7.cloned.1.call-update) | async-done | bytes 196624 | tf_op jit(solution)/shard_map/reduce_scatter | solution.py:38
  63.0 1.1 fusion.22
  64.0 1.1 multiply_reduce_fusion.3
  65.2 1.1 fusion.21
  66.2 8.2 %all_gather.23 = bf16[512,768]{1,0:T(8,128)(2,1)S(1)} all-gather(bf16[128,768]{1,0:T(8,128)(2,1)S(1)} %fusion.21), channel_id=1, replica_groups=mesh['dp'=8,'tensor'=4] {'tensor'}, dimensions={0}, use_global_device_ids=true | all-gather | bytes 983040 | tf_op jit(solution)/shard_map/all_gather | solution.py:44
  74.5 2.0 multiply_convert_fusion.1
  76.5 0.9 copy-done.33
  77.4 1.7 convolution_convert_fusion.3
  79.3 23.6 %reduce-scatter.9.cloned.1.call-done = bf16[128,768]{1,0:T(8,128)(2,1)} async-done(((bf16[512,768]{1,0:T(8,128)(2,1)}), bf16[128,768]{1,0:T(8,128)(2,1)}) %reduce-scatter.9.cloned.1.call-update) | async-done | bytes 196624 | tf_op jit(solution)/shard_map/reduce_scatter | solution.py:38
  102.9 1.2 fusion.31
  104.6 0.9 fusion.29
  105.4 8.2 %all_gather.24 = bf16[512,768]{1,0:T(8,128)(2,1)S(1)} all-gather(bf16[128,768]{1,0:T(8,128)(2,1)S(1)} %get-tuple-element.128), channel_id=1, replica_groups=mesh['dp'=8,'tensor'=4] {'tensor'}, dimensions={0}, use_global_device_ids=true | all-gather | bytes 983040 | tf_op jit(solution)/shard_map/all_gather | solution.py:44
  113.6 1.7 fusion.35
  115.3 0.9 copy-done.34
  116.2 1.7 convolution_convert_fusion.2
  118.0 23.7 %reduce-scatter.11.cloned.1.call-done = bf16[128,768]{1,0:T(8,128)(2,1)} async-done(((bf16[512,768]{1,0:T(8,128)(2,1)}), bf16[128,768]{1,0:T(8,128)(2,1)}) %reduce-scatter.11.cloned.1.call-update) | async-done | bytes 196624 | tf_op jit(solution)/shard_map/reduce_scatter | solution.py:38
  141.7 1.3 multiply_reduce_fusion
  143.0 1.1 fusion.28
  144.2 8.5 %all_gather.25 = bf16[512,768]{1,0:T(8,128)(2,1)S(1)} all-gather(bf16[128,768]{1,0:T(8,128)(2,1)S(1)} %convert_element_type.108), channel_id=1, replica_groups=mesh['dp'=8,'tensor'=4] {'tensor'}, dimensions={0}, use_global_device_ids=true | all-gather | bytes 983040 | tf_op jit(solution)/shard_map/all_gather | solution.py:44
  153.3 1.6 fusion.33
  154.9 1.4 multiply_convert_fusion
  156.3 0.6 convolution_convert_fusion.6
  156.9 1.0 fusion.34
  158.0 0.8 convolution_bitcast_fusion
  159.5 1.3 copy.125
  160.9 2.0 convolution_convert_fusion.1
  163.0 0.8 convolution_convert_fusion
  163.8 1.6 pad_maximum_fusion
  166.9 0.6 reshape.176
  167.6 1.0 pad_maximum_fusion.1
  168.6 0.7 fusion.9
  169.4 1.0 copy.105
  170.4 1.0 reshape.172
  171.4 14.3 %reduce-scatter.13.cloned.1.call-done = bf16[192,528]{1,0:T(8,128)(2,1)} async-done(((bf16[768,528]{1,0:T(8,128)(2,1)}), bf16[192,528]{1,0:T(8,128)(2,1)}) %reduce-scatter.13.cloned.1.call-update) | async-done | bytes 202768
  185.8 0.8 slice.127
  187.2 111.3 %all-reduce.2.cloned.1.call-done = bf16[1536,768]{1,0:T(8,128)(2,1)} async-done(((bf16[1536,768]{1,0:T(8,128)(2,1)}), bf16[1536,768]{1,0:T(8,128)(2,1)}) %all-reduce.2.cloned.1.call-update) | async-done | bytes 2359312 | tf_op jit(solution)/shard_map/psum | solution.py:166
  298.5 1.9 copy.106
  300.6 8.0 %all_to_all.19 = bf16[128,4,192]{0,2,1:T(8,128)(2,1)S(1)} all-to-all(bf16[128,4,192]{0,2,1:T(8,128)(2,1)S(1)} %bitcast.97), channel_id=1, replica_groups=mesh['dp'=8,'tensor'=4] {'tensor'}, dimensions={1} | all-to-all | bytes 393216 | tf_op jit(solution)/shard_map/all_to_all | solution.py:153
  308.6 0.7 copy_bitcast_fusion
  309.5 0.9 copy.110
  310.4 2.5 slice_convert_fusion
  312.9 130.6 %all-gather.8.cloned.1.call-done = bf16[8,3084,192]{1,2,0:T(8,128)(2,1)} async-done(((bf16[1,3084,192]{1,2,0:T(8,128)(2,1)}), bf16[8,3084,192]{1,2,0:T(8,128)(2,1)}) %all-gather.8.cloned.1.call-update) | async-done | bytes 9474064 | tf_op jit(solution)/shard_map/all_gather | solution.py:235
  443.5 5.8 %reduce_sum.192 = bf16[3084,192]{0,1:T(8,128)(2,1)S(1)} reduce(bf16[8,3084,192]{1,2,0:T(8,128)(2,1)} %all-gather.8.cloned.1.call-done, bf16[]{:T(256)} %constant.45.clone.1), dimensions={0}, to_apply=%region_24.25 | reduce | flops 4144896 | bytes 10658306 | tf_op jit(solution)/shard_map/reduce_sum | solution.py:235
  449.4 1.3 slice.128
  450.8 1.6 convert_element_type.111
  452.5 0.7 reshape.179
  453.2 0.7 copy.112
  454.1 1.1 reshape.178
  455.2 1.9 copy.107
  457.2 2.6 reshape.177
  459.8 4.2 copy.111
  464.0 2.4 slice_reduce_fusion
  (133 shorter events, 5.9 us)
Async XLA Ops:
  7.2 67.3 %copy-start = (bf16[768,768]{1,0:T(8,128)(2,1)S(1)}, bf16[768,768]{1,0:T(8,128)(2,1)}, u32[]{:S(2)}) copy-start(bf16[768,768]{1,0:T(8,128)(2,1)} %param.23) | copy-start | bytes 3538948
  7.2 25.4 %all-gather.6.cloned.1.call-start = ((), (), s32[]{:S(2)}) async-start(), calls=%async_computation.5 | async-start | bytes 1966080 | tf_op jit(solution)/shard_map/all_gather | solution.py:97
  9.2 53.8 %reduce-scatter.7.cloned.1.call-start = ((), (), s32[]{:S(2)}) async-start(), calls=%async_computation.6 | async-start | bytes 983040 | tf_op jit(solution)/shard_map/reduce_scatter | solution.py:38
  34.7 1.5 copy-start.14
  35.5 1.7 copy-start.2
  36.2 1.9 copy-start.18
  37.1 1.1 copy-start.7
  38.1 1.5 copy-start.23
  38.2 1.5 copy-start.24
  38.2 1.5 copy-start.25
  38.2 1.4 copy-start.26
  38.2 1.4 copy-start.27
  38.2 1.4 copy-start.28
  39.5 63.3 %reduce-scatter.9.cloned.1.call-start = ((), (), s32[]{:S(2)}) async-start(), calls=%async_computation.7 | async-start | bytes 983040 | tf_op jit(solution)/shard_map/reduce_scatter | solution.py:38
  46.2 28.2 %copy-start.32 = (f32[768]{0:T(1024)S(1)}, f32[768]{0:T(1024)}, u32[]{:S(2)}) copy-start(f32[768]{0:T(1024)} %param.24) | copy-start | bytes 9220
  74.5 2.0 copy-start.9
  74.5 2.9 copy-start.30
  76.5 0.9 copy-start.33
  77.4 25.5 %copy-start.4 = (bf16[128,768]{1,0:T(8,128)(2,1)S(1)}, bf16[128,768]{1,0:T(8,128)(2,1)}, u32[]{:S(2)}) copy-start(bf16[128,768]{1,0:T(8,128)(2,1)} %reduce-scatter.7.cloned.1.call-done) | copy-start | bytes 589828
  79.1 62.7 %reduce-scatter.11.cloned.1.call-start = ((), (), s32[]{:S(2)}) async-start(), calls=%async_computation.8 | async-start | bytes 983040 | tf_op jit(solution)/shard_map/reduce_scatter | solution.py:38
  104.3 9.4 %copy-start.31 = (bf16[768,768]{1,0:T(8,128)(2,1)S(1)}, bf16[768,768]{1,0:T(8,128)(2,1)}, u32[]{:S(2)}) copy-start(bf16[768,768]{1,0:T(8,128)(2,1)} %param.25) | copy-start | bytes 3538948
  104.3 9.4 %copy-start.36 = (f32[512,768]{1,0:T(8,128)S(1)}, f32[512,768]{1,0:T(8,128)}, u32[]{:S(2)}) copy-start(f32[512,768]{1,0:T(8,128)} %get-tuple-element.145) | copy-start | bytes 4718596
  113.6 1.7 copy-start.11
  115.3 0.9 copy-start.34
  117.9 67.8 %reduce-scatter.13.cloned.1.call-start = ((), (), s32[]{:S(2)}) async-start(), calls=%async_computation.11 | async-start | bytes 1228800
  144.2 9.1 %copy-start.3 = (f32[3,512,512]{1,2,0:T(8,128)S(1)}, f32[3,512,512]{1,2,0:T(8,128)}, u32[]{:S(2)}) copy-start(f32[3,512,512]{1,2,0:T(8,128)} %copy-done.2) | copy-start | bytes 9437188
  144.2 9.1 %copy-start.19 = (f32[3,512]{1,0:T(4,128)S(1)}, f32[3,512]{1,0:T(4,128)}, u32[]{:S(2)}) copy-start(f32[3,512]{1,0:T(4,128)} %copy-done.18) | copy-start | bytes 18436
  153.2 1.7 copy-start.15
  154.9 3.1 copy-start.17
  156.3 1.7 copy-start.8
  159.5 1.4 copy-start.12
  160.8 2.1 copy-start.10
  160.8 137.7 %all-reduce.2.cloned.1.call-start = ((), (), s32[]{:S(2)}) async-start(), calls=%async_computation.9 | async-start | bytes 4718592 | tf_op jit(solution)/shard_map/psum | solution.py:166
  160.9 2.1 copy-start.35
  165.3 0.7 copy-start.22
  165.4 1.5 copy-start.20
  165.4 1.5 copy-start.29
  165.4 278.1 %all-gather.8.cloned.1.call-start = ((), (), s32[]{:S(2)}) async-start(), calls=%async_computation.10 | async-start | bytes 11059200 | tf_op jit(solution)/shard_map/all_gather | solution.py:235
  166.1 2.5 copy-start.5
  170.4 16.3 %copy-start.21 = (bf16[1,192]{1,0:T(2,128)(2,1)S(1)}, bf16[1,192]{1,0:T(2,128)(2,1)}, u32[]{:S(2)}) copy-start(bf16[1,192]{1,0:T(2,128)(2,1)} %reshape.176) | copy-start | bytes 1156
  298.5 1.9 copy-start.13
  300.4 8.9 %copy-start.16 = (bf16[192,528]{1,0:T(8,128)(2,1)S(1)}, bf16[192,528]{1,0:T(8,128)(2,1)}, u32[]{:S(2)}) copy-start(bf16[192,528]{1,0:T(8,128)(2,1)} %reduce-scatter.13.cloned.1.call-done) | copy-start | bytes 608260
  300.4 9.9 %copy-start.6 = (bf16[1536,768]{1,0:T(8,128)(2,1)S(1)}, bf16[1536,768]{1,0:T(8,128)(2,1)}, u32[]{:S(2)}) copy-start(bf16[1536,768]{1,0:T(8,128)(2,1)} %all-reduce.2.cloned.1.call-done) | copy-start | bytes 7077892
  457.2 9.2 %copy-start.1 = (bf16[768,768]{1,0:T(8,128)(2,1)S(1)}, bf16[768,768]{1,0:T(8,128)(2,1)}, u32[]{:S(2)}) copy-start(bf16[768,768]{1,0:T(8,128)(2,1)} %param.23) | copy-start | bytes 3538948
Sparse Core Ops, SparseCore 0:
  10.2 22.3 all-gather.5
  39.7 23.2 reduce-scatter.6
  79.2 23.6 reduce-scatter.8
  118.0 23.6 reduce-scatter.10
  160.9 24.7 reduce-scatter.12
  189.8 108.7 all-reduce.1
  301.5 141.8 all-gather.7
